TPU v7x, 32 devices: a whole 2x2x4 slice. The times are simulated.
32 devices in a mesh: gx: 8 (over z, y), gy: 4 (over x, core).
Axes of the slice: x: 2, y: 2, z: 4, core: 2. Of those that a mesh axis runs over, the one named last changes fastest.
Arguments:
- right_side: float32 [16, 512, 1024], P(None, 'gx', 'gy'), may hold values from -50 to 50
- center: float32 [512, 1024], P('gx', 'gy'), may hold values from 4 to 6
- couplings: float32 [4, 512, 1024], P(None, 'gx', 'gy'), may hold values from 0.1 to 1
Outputs:
- q_basis: float32 [80, 512, 1024], P(None, 'gx', 'gy')
- r_factor: float32 [80, 80], replicated
All inputs are finite; a program needn't handle non-finite values.
Results may differ from a plain program's by a relative error of at most 0.0003.
Values sent between devices are 32-bit elements; how exact they have to be, the bound alone decides.
A program may use at most 64 MiB of HBM per device.

v0:
```python
import math

import jax
import jax.numpy as jnp
from jax import lax
from jax.sharding import PartitionSpec as P

S = 4


def with_halo(cells, sides, width):
    for axis, dim in sides:
        count = lax.axis_size(axis)
        ends = count - 1
        head = lax.slice_in_dim(cells, 0, width, axis=dim)
        tail = lax.slice_in_dim(cells, cells.shape[dim] - width, cells.shape[dim], axis=dim)
        cells = jnp.concatenate(
            [
                lax.ppermute(tail, axis, [(i, (i + 1) % count) for i in range(ends)]),
                cells,
                lax.ppermute(head, axis, [((i + 1) % count, i) for i in range(ends)]),
            ],
            axis=dim,
        )
    return cells


def stencil(padded, shifted, couplings):
    middle = padded[:, 1:-1, 1:-1]
    nearby = couplings[0] * padded[:, :-2, 1:-1] + couplings[1] * padded[:, 2:, 1:-1]
    nearby = nearby + couplings[2] * padded[:, 1:-1, :-2]
    nearby = nearby + couplings[3] * padded[:, 1:-1, 2:]
    return shifted * middle - nearby


def cholesky_upper(gram_matrix):
    order = gram_matrix.shape[0]
    positions = jnp.arange(order, dtype=jnp.int32)

    def column_step(index, lower):
        picker = (positions == index).astype(gram_matrix.dtype)
        row_vals = jnp.dot(picker, lower, precision=lax.Precision.HIGHEST)
        remain = jnp.dot(gram_matrix, picker, precision=lax.Precision.HIGHEST) - jnp.dot(
            lower, row_vals, precision=lax.Precision.HIGHEST
        )
        pivot = jnp.sqrt(jnp.sum(remain * picker))
        column = jnp.where(positions >= index, remain / pivot, jnp.zeros_like(remain))
        return lower + column[:, None] * picker[None, :]

    lower = lax.fori_loop(0, order, column_step, jnp.zeros_like(gram_matrix))
    return lower.T


def upper_inverse(upper_factor):
    order = upper_factor.shape[0]
    positions = jnp.arange(order, dtype=jnp.int32)

    def row_step(count, inverse):
        index = order - 1 - count
        picker = (positions == index).astype(upper_factor.dtype)
        row_vals = jnp.dot(picker, upper_factor, precision=lax.Precision.HIGHEST)
        pivot = jnp.sum(row_vals * picker)
        solved = (picker - jnp.dot(row_vals, inverse, precision=lax.Precision.HIGHEST)) / pivot
        return inverse + picker[:, None] * solved[None, :]

    return lax.fori_loop(0, order, row_step, jnp.zeros_like(upper_factor))


def triangle_pair(gram_matrix):
    upper_factor = cholesky_upper(gram_matrix)
    return (upper_factor, upper_inverse(upper_factor))


def inner_products(matrix):
    return jnp.dot(matrix, matrix.T, precision=lax.Precision.HIGHEST)


def tall_factor(matrix):
    upper_one, inverse_one = triangle_pair(inner_products(matrix))
    first_pass = jnp.dot(inverse_one.T, matrix, precision=lax.Precision.HIGHEST)
    upper_two = cholesky_upper(inner_products(first_pass))
    return jnp.dot(upper_two, upper_one, precision=lax.Precision.HIGHEST)


def on_device(right_side, center, couplings):
    shifted = center - 5.0
    tile_rows, tile_cols = shifted.shape
    blocks = [right_side]
    for power in range(S):
        padded = with_halo(blocks[-1], (("gx", 1), ("gy", 2)), 1)
        blocks.append(stencil(padded, shifted, couplings))
    local_basis = jnp.concatenate(blocks, 0).reshape(-1, tile_rows * tile_cols)
    basis_width = local_basis.shape[0]
    cell_total = tile_rows * tile_cols * lax.axis_size("gx") * lax.axis_size("gy")
    norm_scale = math.sqrt(cell_total)
    leaf_factor = tall_factor(local_basis)
    gathered = lax.all_gather(leaf_factor[None], ("gx", "gy"), axis=0, tiled=True)
    upper_factor = tall_factor(gathered.reshape(-1, basis_width).T)
    inverse = upper_inverse(upper_factor)
    ortho = jnp.dot(inverse.T, local_basis, precision=lax.Precision.HIGHEST)
    q_local = (ortho * norm_scale).reshape(basis_width, tile_rows, tile_cols)
    return (q_local, upper_factor / norm_scale)


def solution(mesh):
    placed = (P(None, "gx", "gy"), P("gx", "gy"), P(None, "gx", "gy"))
    return jax.shard_map(
        on_device, mesh=mesh, in_specs=placed, out_specs=(P(None, "gx", "gy"), P()), check_vma=False
    )
```

profile of v0, /device:TPU:0, one launch (start us, length us, event | category | flops | bytes accessed | tf_op | source)
XLA Modules:
  0.0 1175.3 jit_solution(10356851370586733047)
XLA Ops:
  2.6 4.9 collective-permute-start
  23.0 2.9 constant_dynamic-update-slice_fusion.5
  25.9 4.3 collective-permute-start.4
  31.6 4.2 collective-permute-done.5
  36.4 2.9 collective-permute-start.6
  46.5 3.4 collective-permute-start.8
  51.4 4.2 collective-permute-done.9
  56.1 2.9 collective-permute-start.10
  66.2 4.3 collective-permute-start.12
  72.0 4.2 collective-permute-done.13
  76.8 2.9 collective-permute-start.14
  86.0 8.5 convolution_bitcast_fusion.15
  97.4 145.6 %while.105 = (s32[]{:T(128)}, f32[80,80]{1,0:T(8,128)S(1)}, f32[80,80]{1,0:T(8,128)S(1)}, s32[]{:T(128)}, s32[]{:T(128)}) while((s32[]{:T(128)}, f32[80,80]{1,0:T(8,128)S(1)}, f32[80,80]{1,0:T(8,128)S(1)}, s32[]{:T(128)}, s32[]{:T(128)}) %tuple.253), condition=%wide.region_2.3_spmd.clone.clone, body=%wide.region_0.2_spmd.clone.clone.sunk | while | flops 263282 | bytes 131309 | solution.py:50
  243.0 131.2 %while.102 = (s32[]{:T(128)}, f32[80,80]{1,0:T(8,128)S(1)}, f32[80,80]{1,0:T(8,128)S(1)}, s32[]{:T(128)}, s32[]{:T(128)}, /*index=5*/s32[]{:T(128)}) while((s32[]{:T(128)}, f32[80,80]{1,0:T(8,128)S(1)}, f32[80,80]{1,0:T(8,128)S(1)}, s32[]{:T(128)}, s32[]{:T(128)}, /*index=5*/s32[]{:T(128)}) %tuple.256), condition=%wide.region_5.6_spmd.clone, body=%wide.region_3.5_spmd.clone.sunk | while | flops 180003 | bytes 104432 | solution.py:66
  374.2 6.7 fusion.158
  381.0 4.2 fusion.159
  385.2 157.9 %while.106 = (s32[]{:T(128)}, f32[80,80]{1,0:T(8,128)S(1)}, f32[80,80]{1,0:T(8,128)S(1)}, s32[]{:T(128)}, s32[]{:T(128)}) while((s32[]{:T(128)}, f32[80,80]{1,0:T(8,128)S(1)}, f32[80,80]{1,0:T(8,128)S(1)}, s32[]{:T(128)}, s32[]{:T(128)}) %tuple.259), condition=%wide.region_8.9_spmd.clone.clone, body=%wide.region_6.8_spmd.clone.clone.sunk | while | flops 263282 | bytes 131309 | solution.py:50
  543.4 42.4 %all-gather = f32[2560,80]{1,0:T(8,128)S(1)} all-gather(f32[80,80]{1,0:T(8,128)S(1)} %fusion.160), channel_id=2, replica_groups=mesh['gx'=8,'gy'=4] {'gx','gy'}, dimensions={0}, use_global_device_ids=true | all-gather | bytes 844800 | tf_op jit(solution)/shard_map/all_gather | solution.py:97
  588.0 146.6 %while.107 = (s32[]{:T(128)}, f32[80,80]{1,0:T(8,128)S(1)}, f32[80,80]{1,0:T(8,128)S(1)}, s32[]{:T(128)}, s32[]{:T(128)}) while((s32[]{:T(128)}, f32[80,80]{1,0:T(8,128)S(1)}, f32[80,80]{1,0:T(8,128)S(1)}, s32[]{:T(128)}, s32[]{:T(128)}) %tuple.262), condition=%wide.region_11.12_spmd.clone.clone, body=%wide.region_9.11_spmd.clone.clone.sunk | while | flops 263282 | bytes 131309 | solution.py:50
  734.7 141.9 %while.103 = (s32[]{:T(128)}, f32[80,80]{1,0:T(8,128)S(1)}, f32[80,80]{1,0:T(8,128)S(1)}, s32[]{:T(128)}, s32[]{:T(128)}, /*index=5*/s32[]{:T(128)}) while((s32[]{:T(128)}, f32[80,80]{1,0:T(8,128)S(1)}, f32[80,80]{1,0:T(8,128)S(1)}, s32[]{:T(128)}, s32[]{:T(128)}, /*index=5*/s32[]{:T(128)}) %tuple.265), condition=%wide.region_14.15_spmd.clone, body=%wide.region_12.14_spmd.clone.sunk | while | flops 180003 | bytes 104432 | solution.py:66
  879.0 153.1 %while.108 = (s32[]{:T(128)}, f32[80,80]{1,0:T(8,128)S(1)}, f32[80,80]{1,0:T(8,128)S(1)}, s32[]{:T(128)}, s32[]{:T(128)}) while((s32[]{:T(128)}, f32[80,80]{1,0:T(8,128)S(1)}, f32[80,80]{1,0:T(8,128)S(1)}, s32[]{:T(128)}, s32[]{:T(128)}) %tuple.268), condition=%wide.region_17.18_spmd.clone.clone, body=%wide.region_15.17_spmd.clone.clone.sunk | while | flops 263282 | bytes 131309 | solution.py:50
  1032.9 131.6 %while.104 = (s32[]{:T(128)}, f32[80,80]{1,0:T(8,128)S(1)}, f32[80,80]{1,0:T(8,128)S(1)}, s32[]{:T(128)}, s32[]{:T(128)}, /*index=5*/s32[]{:T(128)}) while((s32[]{:T(128)}, f32[80,80]{1,0:T(8,128)S(1)}, f32[80,80]{1,0:T(8,128)S(1)}, s32[]{:T(128)}, s32[]{:T(128)}, /*index=5*/s32[]{:T(128)}) %tuple.271), condition=%wide.region_20.21_spmd.clone, body=%wide.region_18.20_spmd.clone.sunk | while | flops 180003 | bytes 104432 | solution.py:66
  1164.5 6.8 convolution_multiply_fusion
  1171.4 3.9 copy.55
  (2965 shorter events, 835.7 us)
Async XLA Ops:
  0.6 8.3 copy-start.1
  0.6 8.1 copy-start.4
  2.6 6.3 collective-permute-start
  7.5 5.6 collective-permute-start.1
  8.8 14.1 %copy-start.2 = (f32[64,256]{1,0:T(8,128)}, f32[64,256]{1,0:T(8,128)S(1)}, u32[]{:S(2)}) copy-start(f32[64,256]{1,0:T(8,128)S(1)} %get-tuple-element.821) | copy-start | bytes 196612
  13.1 5.2 copy-start.5
  15.5 2.9 collective-permute-start.2
  17.0 4.8 collective-permute-start.3
  25.9 5.7 collective-permute-start.4
  30.2 5.6 collective-permute-start.5
  36.4 4.5 collective-permute-start.6
  39.6 4.0 collective-permute-start.7
  46.5 4.8 collective-permute-start.8
  49.9 5.6 collective-permute-start.9
  56.1 4.5 collective-permute-start.10
  59.3 4.0 collective-permute-start.11
  66.2 5.7 collective-permute-start.12
  70.6 5.6 collective-permute-start.13
  76.5 7.8 copy-start.3
  76.8 4.7 collective-permute-start.14
  79.9 4.0 collective-permute-start.15
  86.0 8.5 copy-start
where the time goes:
time: 1180 us
  matrix products  765 us (65%)
  loops' own time  225 us (19%)
  other arithmetic  59.7 us (5%)
  blocking collectives  42.4 us (4%)
  starting transfers between devices  37.3 us (3%)
  waiting for transfers between devices  24.9 us (2%)
  local copies, waits for them, and re-layouts  19.8 us (2%)
    dot_general x320, matrix products, column_step(): jnp.dot(lower, row_vals, precision=lax.Precision.HIGHEST)  274 us
    another operation x4, loops' own time, cholesky_upper(): lower = lax.fori_loop(0, order, column_step, jnp.zeros_like(gram_matrix))  217 us
    dot_general x240, matrix products, row_step(): row_vals = jnp.dot(picker, upper_factor, precision=lax.Precision.HIGHEST)  190 us
    dot_general x240, matrix products, row_step(): jnp.dot(row_vals, inverse, precision=lax.Precision.HIGHEST)  186 us
    all_gather x1, blocking collectives, on_device(): lax.all_gather(leaf_factor[None], ('gx', 'gy'), axis=0, tiled=True)  42.4 us
    dot_general x320, matrix products, column_step(): jnp.dot(gram_matrix, picker, precision=lax.Precision.HIGHEST)  41.9 us
    dot_general x320, matrix products, column_step(): row_vals = jnp.dot(picker, lower, precision=lax.Precision.HIGHEST)  41.4 us
    ppermute x8, starting transfers between devices, with_halo(): lax.ppermute(tail, axis, [(i, (i + 1) % count) for i in range(ends)])  26.8 us
  transfers between devices with their start and end apart: 16, of which 12 were waited for; matrix products, arithmetic and copies ran while one was open for 0% of the time, Pallas kernels for 0%

commit v1 on v0

v1 whole, which is shorter than its diff:
```python
import functools
import math

import jax
import jax.numpy as jnp
from jax import lax
from jax.experimental import pallas as pl
from jax.experimental.pallas import tpu as pltpu
from jax.sharding import PartitionSpec as P

S = 4
B = 16
COLS = B * (S + 1)
F32 = jnp.float32
BF16 = jnp.bfloat16
MESH = pl.DeviceIdType.MESH
VMEM_LIMIT = 56 * 1024 * 1024


def split(x, count):
    parts = []
    for _ in range(count - 1):
        part = x.astype(BF16)
        parts.append(part)
        x = x - part.astype(F32)
    parts.append(x.astype(BF16))
    return parts


def dot(a, b):
    return jnp.dot(a, b, preferred_element_type=F32)


def dot_nt(a, b):
    return lax.dot_general(a, b, (((1,), (1,)), ((), ())), preferred_element_type=F32)


def exchange(cells, axis, dim, width):
    count = lax.axis_size(axis)
    ends = count - 1
    size = cells.shape[dim]
    head = lax.slice_in_dim(cells, 0, width, axis=dim)
    tail = lax.slice_in_dim(cells, size - width, size, axis=dim)
    before = lax.ppermute(tail, axis, [(i, i + 1) for i in range(ends)])
    after = lax.ppermute(head, axis, [(i + 1, i) for i in range(ends)])
    return before, after


def powers_kernel(rows, cols, chunk, padded, basis, gram, held, acc, levels):
    step = pl.program_id(0)

    def apply(power, r):
        if power == 1:
            def src(i):
                return padded[i, 0:B, :]
        else:
            def src(i):
                return levels[(power - 1) % 2, i]
        here = src(r)
        width = here.shape[1]

        def coef(j):
            return padded[r, B + j : B + j + 1, :]

        near = coef(1) * src(r - 1) + coef(2) * src(r + 1)
        near = near + coef(3) * pltpu.roll(here, 1, 1)
        near = near + coef(4) * pltpu.roll(here, width - 1, 1)
        return coef(0) * here - near

    @pl.when(step == 0)
    def _():
        acc[...] = jnp.zeros_like(acc)

        def copy_row(r, carry):
            held[r, 0:B, :] = padded[r + S, 0:B, 0:cols]
            return carry

        lax.fori_loop(0, rows, copy_row, 0, unroll=4)
        for power in range(1, S + 1):
            for r in list(range(power, S)) + list(range(rows + S, rows + 2 * S - power)):
                levels[power % 2, r] = apply(power, r)

            def row(r, carry):
                out = apply(power, r + S)
                if power < S:
                    levels[power % 2, r + S] = out
                held[r, B * power : B * power + B, :] = out[:, 0:cols]
                return carry

            lax.fori_loop(0, rows, row, 0, unroll=4)

    basis[...] = held[pl.ds(step * chunk, chunk)]
    part = None
    for j in range(0, chunk, 4):
        wide = jnp.concatenate([held[step * chunk + j + i] for i in range(4)], axis=1)
        stack = jnp.concatenate(split(wide, 3), axis=0)
        add = dot_nt(stack, stack)
        part = add if part is None else part + add
    acc[...] += part

    @pl.when(step == pl.num_programs(0) - 1)
    def _():
        a = acc[...]
        c = COLS

        def block(i, j):
            return a[i * c : i * c + c, j * c : j * c + c]

        small = block(0, 2) + block(2, 0) + block(1, 1)
        total = block(0, 0) + ((block(0, 1) + block(1, 0)) + small)
        gram[...] = jnp.zeros_like(gram)
        gram[0:c, 0:c] = total


def powers(padded, rows, cols, pad_rows):
    chunk = 8
    return pl.pallas_call(
        functools.partial(powers_kernel, rows, cols, chunk),
        grid=(rows // chunk,),
        in_specs=[pl.BlockSpec(padded.shape, lambda i: (0, 0, 0))],
        out_specs=[
            pl.BlockSpec((chunk, COLS, cols), lambda i: (i, 0, 0)),
            pl.BlockSpec((pad_rows, 128), lambda i: (0, 0)),
        ],
        out_shape=[
            jax.ShapeDtypeStruct((rows, COLS, cols), F32),
            jax.ShapeDtypeStruct((pad_rows, 128), F32),
        ],
        scratch_shapes=[
            pltpu.VMEM((rows, COLS, cols), F32),
            pltpu.VMEM((3 * COLS, 3 * COLS), F32),
            pltpu.VMEM((2, padded.shape[0], B, padded.shape[2]), F32),
        ],
        compiler_params=pltpu.CompilerParams(vmem_limit_bytes=VMEM_LIMIT),
        name="powers",
    )(padded)


def total_kernel(nx, ny, piece, x_ref, out_ref, got_row, got_col, send, r1, r2, r3):
    gx, gy = lax.axis_index("gx"), lax.axis_index("gy")
    barrier = pltpu.get_barrier_semaphore()
    rows = [(gx, lax.rem(gy + d, ny)) for d in range(1, ny)]
    columns = [(lax.rem(gx + d, nx), gy) for d in range(1, nx)]
    for peer in rows + columns:
        pl.semaphore_signal(barrier, inc=1, device_id=peer, device_id_type=MESH)
    pl.semaphore_wait(barrier, len(rows) + len(columns))

    def push(src, dst, index, sem, peer):
        copy = pltpu.make_async_remote_copy(
            src_ref=src, dst_ref=dst, send_sem=send.at[index], recv_sem=sem,
            device_id=peer, device_id_type=MESH,
        )
        copy.start()
        return copy

    def part(i):
        return pl.ds(pl.multiple_of(i * piece, 8), piece)

    copies = [
        push(x_ref.at[part(peer[1])], got_row.at[gy], i, r1.at[i], peer)
        for i, peer in enumerate(rows)
    ]
    got_row[gy] = x_ref[part(gy)]
    for copy in copies:
        copy.wait()
    held = got_row[0]
    for i in range(1, ny):
        held = held + got_row[i]
    got_col[gx] = held
    copies = [
        push(got_col.at[gx], got_col.at[gx], i, r2.at[i], peer) for i, peer in enumerate(columns)
    ]
    for copy in copies:
        copy.wait()
    held = got_col[0]
    for i in range(1, nx):
        held = held + got_col[i]
    out_ref[part(gy)] = held
    copies = [
        push(out_ref.at[part(gy)], out_ref.at[part(gy)], i, r3.at[i], peer)
        for i, peer in enumerate(rows)
    ]
    for copy in copies:
        copy.wait()


def total(x, nx, ny, ident):
    piece = x.shape[0] // ny
    most = max(nx, ny) - 1
    return pl.pallas_call(
        functools.partial(total_kernel, nx, ny, piece),
        in_specs=[pl.BlockSpec(memory_space=pltpu.VMEM)],
        out_specs=pl.BlockSpec(memory_space=pltpu.VMEM),
        out_shape=jax.ShapeDtypeStruct(x.shape, F32),
        scratch_shapes=[
            pltpu.VMEM((ny, piece, 128), F32),
            pltpu.VMEM((nx, piece, 128), F32),
            pltpu.SemaphoreType.DMA((most,)),
            pltpu.SemaphoreType.DMA((max(ny - 1, 1),)),
            pltpu.SemaphoreType.DMA((max(nx - 1, 1),)),
            pltpu.SemaphoreType.DMA((max(ny - 1, 1),)),
        ],
        compiler_params=pltpu.CompilerParams(collective_id=ident, has_side_effects=True),
        name="total",
    )(x)


def eliminate(gram):
    c = COLS
    row_id = lax.broadcasted_iota(jnp.int32, (c, 128), 0)
    lane_id = lax.broadcasted_iota(jnp.int32, (c, 128), 1)
    work = jnp.concatenate([gram, (row_id == lane_id).astype(F32)], axis=1)
    tiles = [work[8 * t : 8 * t + 8] for t in range(c // 8)]
    sub = lax.broadcasted_iota(jnp.int32, (8, 1), 0)
    for k in range(c):
        t0, s0 = divmod(k, 8)
        row = tiles[t0][s0 : s0 + 1]
        pivot = row[:, k : k + 1]
        scale = 1.0 / jnp.sqrt(pivot)
        row = row * scale
        for t in range(t0, c // 8):
            mult = tiles[t][:, k : k + 1] * scale
            if t == t0:
                mult = jnp.where(sub > s0, mult, 0.0)
                tiles[t] = jnp.where(sub == s0, row, tiles[t] - mult * row)
            else:
                tiles[t] = tiles[t] - mult * row
    done = jnp.concatenate(tiles, axis=0)
    upper = jnp.where(lane_id >= row_id, done[:, 0:128], 0.0)
    return upper, done[:, 128:256]


def spread(parts):
    wide = None
    for i, part in enumerate(parts):
        one = jnp.concatenate([part.astype(F32), jnp.zeros_like(part, F32)], axis=1)
        if i:
            one = pltpu.roll(one, COLS * i, 1)
        wide = one if wide is None else wide + one
    return wide.astype(BF16)


def first_kernel(chunk, gram, basis, upper_ref, high, low, gram_out, left, acc):
    step = pl.program_id(0)

    @pl.when(step == 0)
    def _():
        acc[...] = jnp.zeros_like(acc)
        upper, inverse = eliminate(gram[0:COLS, :])
        upper_ref[...] = upper
        a, b, c = split(inverse, 3)
        left[0] = spread([a, b, a])
        left[1] = spread([c, b, a])

    pad = jnp.zeros((256 - 3 * COLS, basis.shape[2]), BF16)
    part = None
    for j in range(chunk):
        a, b, c = split(basis[j], 3)
        q = dot(left[0], jnp.concatenate([a, a, b, pad], axis=0))
        q = q + dot(left[1], jnp.concatenate([a, b, c, pad], axis=0))
        hi, lo = split(q, 2)
        high[j] = hi
        low[j] = lo
        stack = jnp.concatenate([hi, lo], axis=0)
        add = dot_nt(stack, stack)
        part = add if part is None else part + add
    acc[...] += part

    @pl.when(step == pl.num_programs(0) - 1)
    def _():
        c = COLS
        a = acc[...]
        gram_out[...] = jnp.zeros_like(gram_out)
        gram_out[0:c, 0:c] = a[0:c, 0:c] + (
            (a[0:c, c : 2 * c] + a[c : 2 * c, 0:c]) + a[c : 2 * c, c : 2 * c]
        )


def first(gram, basis):
    rows, _, cols = basis.shape
    chunk = 8
    return pl.pallas_call(
        functools.partial(first_kernel, chunk),
        grid=(rows // chunk,),
        in_specs=[
            pl.BlockSpec(gram.shape, lambda i: (0, 0)),
            pl.BlockSpec((chunk, COLS, cols), lambda i: (i, 0, 0)),
        ],
        out_specs=[
            pl.BlockSpec((COLS, 128), lambda i: (0, 0)),
            pl.BlockSpec((chunk, COLS, cols), lambda i: (i, 0, 0)),
            pl.BlockSpec((chunk, COLS, cols), lambda i: (i, 0, 0)),
            pl.BlockSpec(gram.shape, lambda i: (0, 0)),
        ],
        out_shape=[
            jax.ShapeDtypeStruct((COLS, 128), F32),
            jax.ShapeDtypeStruct((rows, COLS, cols), BF16),
            jax.ShapeDtypeStruct((rows, COLS, cols), BF16),
            jax.ShapeDtypeStruct(gram.shape, F32),
        ],
        scratch_shapes=[
            pltpu.VMEM((2, COLS, 256), BF16),
            pltpu.VMEM((2 * COLS, 2 * COLS), F32),
        ],
        compiler_params=pltpu.CompilerParams(vmem_limit_bytes=VMEM_LIMIT),
        name="first",
    )(gram, basis)


def second_kernel(chunk, norm, gram, upper_one, high, low, q_ref, r_ref, left):
    step = pl.program_id(0)

    @pl.when(step == 0)
    def _():
        upper, inverse = eliminate(gram[0:COLS, :])
        full = jnp.dot(
            upper[:, 0:COLS], upper_one[...], precision=lax.Precision.HIGHEST,
            preferred_element_type=F32,
        )
        r_ref[...] = full[:, 0:COLS] / norm
        a, b = split(inverse * norm, 2)
        left[...] = spread([a, b, a])

    pad = jnp.zeros((256 - 3 * COLS, high.shape[2]), BF16)
    out = []
    for j in range(chunk):
        hi, lo = high[j], low[j]
        out.append(dot(left[...], jnp.concatenate([hi, hi, lo, pad], axis=0)))
    q_ref[...] = jnp.swapaxes(jnp.stack(out, 0), 0, 1)


def second(gram, upper_one, high, low, norm):
    rows, _, cols = high.shape
    chunk = 8
    return pl.pallas_call(
        functools.partial(second_kernel, chunk, norm),
        grid=(rows // chunk,),
        in_specs=[
            pl.BlockSpec(gram.shape, lambda i: (0, 0)),
            pl.BlockSpec(upper_one.shape, lambda i: (0, 0)),
            pl.BlockSpec((chunk, COLS, cols), lambda i: (i, 0, 0)),
            pl.BlockSpec((chunk, COLS, cols), lambda i: (i, 0, 0)),
        ],
        out_specs=[
            pl.BlockSpec((COLS, chunk, cols), lambda i: (0, i, 0)),
            pl.BlockSpec((COLS, COLS), lambda i: (0, 0)),
        ],
        out_shape=[
            jax.ShapeDtypeStruct((COLS, rows, cols), F32),
            jax.ShapeDtypeStruct((COLS, COLS), F32),
        ],
        scratch_shapes=[pltpu.VMEM((COLS, 256), BF16)],
        compiler_params=pltpu.CompilerParams(vmem_limit_bytes=VMEM_LIMIT),
        name="second",
    )(gram, upper_one, high, low)


def on_device(nx, ny, right_side, center, couplings):
    rows, cols = center.shape
    norm = math.sqrt(rows * cols * nx * ny)
    fields = jnp.concatenate(
        [right_side, (center - 5.0)[None], couplings, jnp.zeros((3, rows, cols), F32)], 0
    )
    fields = jnp.swapaxes(fields, 0, 1)
    up, down = exchange(fields, "gx", 0, S)
    fields = jnp.concatenate([up, fields, down], 0)
    left, right = exchange(fields, "gy", 2, S)
    gap = jnp.zeros(fields.shape[:2] + (128 - 2 * S,), F32)
    padded = jnp.concatenate([fields, right, gap, left], 2)

    pad_rows = -(-COLS // (8 * ny)) * 8 * ny
    basis, gram = powers(padded, rows, cols, pad_rows)
    gram = total(gram, nx, ny, 1)
    upper_one, high, low, gram = first(gram, basis)
    gram = total(gram, nx, ny, 1)
    return second(gram, upper_one, high, low, norm)


def solution(mesh):
    placed = (P(None, "gx", "gy"), P("gx", "gy"), P(None, "gx", "gy"))
    return jax.shard_map(
        functools.partial(on_device, mesh.shape["gx"], mesh.shape["gy"]),
        mesh=mesh, in_specs=placed, out_specs=(P(None, "gx", "gy"), P()), check_vma=False,
    )
```

time: 1180 us -> 110 us (0.09)
  matrix products: 765 us -> 0 us
  loops' own time: 225 us -> 0 us
  Pallas kernels: 0 us -> 82.2 us
  other arithmetic: 59.7 us -> 3.06 us
  blocking collectives: 42.4 us -> 0 us
  starting transfers between devices: 37.3 us -> 11.1 us
  waiting for transfers between devices: 24.9 us -> 5.22 us
  local copies, waits for them, and re-layouts: 19.8 us -> 6.32 us
    dot_general x1449 -> x0, matrix products: 765 us -> none  [the longest x320 274 us: column_step(): jnp.dot(lower, row_vals, precision=lax.Precision.HIGHEST)]
    another operation x7 -> x0, loops' own time: 225 us -> none  [the longest x4 217 us: cholesky_upper(): lower = lax.fori_loop(0, order, column_step, jnp.zeros_like(gram_matrix))]
    pallas_call x0 -> x5, Pallas kernels: none -> 82.2 us  [the longest x2 30.9 us: total(): pl.pallas_call(functools.partial(total_kernel, nx, ny, piece), in_specs=[...]
    add x560 -> x0, other arithmetic: 45.9 us -> none  [the longest x320 25.3 us: column_step(): return lower + column[:, None] * picker[None, :]]
    all_gather x1 -> x0, blocking collectives: 42.4 us -> none  [on_device(): lax.all_gather(leaf_factor[None], ('gx', 'gy'), axis=0, tiled=True)]
    ppermute x16 -> x4, starting transfers between devices: 37.3 us -> 11.1 us  [the longest x2 8.52 us: exchange(): before = lax.ppermute(tail, axis, [(i, i + 1) for i in range(ends)])]
    ppermute x16 -> x4, waiting for transfers between devices: 24.9 us -> 5.22 us  [the longest x2 4.32 us: exchange(): after = lax.ppermute(head, axis, [(i + 1, i) for i in range(ends)])]
  transfers between devices with their start and end apart: 16 -> 4, of which waited for: 12 -> 2; matrix products, arithmetic and copies ran while one was open for 0% -> 1% of each run, Pallas kernels for 0% -> 0%
where the time goes in v1:
time: 110 us; the launch traced here: 109 us
  Pallas kernels  82.2 us (75%)
  starting transfers between devices  11.1 us (10%)
  local copies, waits for them, and re-layouts  6.32 us (6%)
  waiting for transfers between devices  5.22 us (5%)
  other arithmetic  3.06 us (3%)
    pallas_call x2, Pallas kernels, total(): pl.pallas_call(functools.partial(total_kernel, nx, ny, piece), in_specs=[...  30.9 us
    pallas_call x1, Pallas kernels, first(): pl.pallas_call(functools.partial(first_kernel, chunk), grid=(rows // chun...  19.1 us
    pallas_call x1, Pallas kernels, powers(): pl.pallas_call(functools.partial(powers_kernel, rows, cols, chunk), grid=...  16.1 us
    pallas_call x1, Pallas kernels, second(): pl.pallas_call(functools.partial(second_kernel, chunk, norm), grid=(rows...  16.1 us
    ppermute x2, starting transfers between devices, exchange(): before = lax.ppermute(tail, axis, [(i, i + 1) for i in range(ends)])  8.52 us
    ppermute x2, waiting for transfers between devices, exchange(): after = lax.ppermute(head, axis, [(i + 1, i) for i in range(ends)])  4.32 us
    unnamed x2, local copies, waits for them, and re-layouts  2.96 us
    ppermute x2, starting transfers between devices, exchange(): after = lax.ppermute(head, axis, [(i + 1, i) for i in range(ends)])  2.57 us
  transfers between devices with their start and end apart: 4, of which 2 were waited for; matrix products, arithmetic and copies ran while one was open for 1% of the time, Pallas kernels for 0%

profile of v1, /device:TPU:0, one launch (start us, length us, event | category | flops | bytes accessed | tf_op | source)
XLA Modules:
  0.0 108.6 jit_solution(5493096821363021546)
XLA Ops:
  0.6 0.8 broadcast_add_fusion
  1.5 1.1 %copy.8 = f32[4,64,256]{2,0,1:T(4,128)S(1)} copy(f32[4,64,256]{2,1,0:T(8,128)} %param.5) | data formatting | bytes 524288 | tf_op args[2]
  2.7 1.8 %copy.7 = f32[16,64,256]{2,0,1:T(8,128)S(1)} copy(f32[16,64,256]{2,1,0:T(8,128)} %param.3) | data formatting | bytes 2097152 | tf_op args[0]
  4.5 0.1 pad.12.clone
  4.6 0.2 maximum_bitcast_fusion
  4.8 4.9 %collective-permute-start = (f32[4,24,256]{2,1,0:T(8,128)S(1)}, f32[4,24,256]{2,1,0:T(8,128)S(1)}, u32[]{:S(2)}, u32[]{:S(2)}) collective-permute-start(f32[4,24,256]{2,1,0:T(8,128)S(1)} %get-tuple-element.16), channel_id=1, source_target_pairs={{0,4},{4,8},{8,12},{12,16},{16,20},{20,24},{24,28},{1,5},{5,9},{9,... | collective-permute-start | bytes 294920 | tf_op jit(solution)/shard_map/ppermute | solution.py:44
  9.7 1.3 %collective-permute-start.1 = (f32[4,24,256]{2,1,0:T(8,128)S(1)}, f32[4,24,256]{2,1,0:T(8,128)S(1)}, u32[]{:S(2)}, u32[]{:S(2)}) collective-permute-start(f32[4,24,256]{2,1,0:T(8,128)S(1)} %get-tuple-element.17), channel_id=1, source_target_pairs={{4,0},{8,4},{12,8},{16,12},{20,16},{24,20},{28,24},{5,1},{9,5},{13... | collective-permute-start | bytes 294920 | tf_op jit(solution)/shard_map/ppermute | solution.py:45
  11.0 0.9 collective-permute-done
  11.9 4.3 %collective-permute-done.1 = f32[4,24,256]{2,1,0:T(8,128)S(1)} collective-permute-done((f32[4,24,256]{2,1,0:T(8,128)S(1)}, f32[4,24,256]{2,1,0:T(8,128)S(1)}, u32[]{:S(2)}, u32[]{:S(2)}) %collective-permute-start.1) | collective-permute-done | bytes 98336 | tf_op jit(solution)/shard_map/ppermute | solution.py:45
  16.2 0.1 pad_maximum_fusion.1
  16.3 0.3 fusion
  16.6 1.0 copy.9
  17.6 1.3 %collective-permute-start.2 = (f32[72,24,4]{0,1,2:T(8,128)}, f32[72,24,4]{0,1,2:T(8,128)S(1)}, u32[]{:S(2)}, u32[]{:S(2)}) collective-permute-start(f32[72,24,4]{0,1,2:T(8,128)} %copy.9), channel_id=1, source_target_pairs={{1,0},{2,1},{3,2},{5,4},{6,5},{7,6},{9,8},{10,9},{11,10},{13,12},{... | collective-permute-start | bytes 82952 | tf_op jit(solution)/shard_map/ppermute | solution.py:45
  18.9 0.3 copy.10
  19.2 3.6 %collective-permute-start.3 = (f32[72,24,4]{0,1,2:T(8,128)S(1)}, f32[72,24,4]{0,1,2:T(8,128)}, u32[]{:S(2)}, u32[]{:S(2)}) collective-permute-start(f32[72,24,4]{0,1,2:T(8,128)S(1)} %copy.10), channel_id=1, source_target_pairs={{0,1},{1,2},{2,3},{4,5},{5,6},{6,7},{8,9},{9,10},{10,11},{12,13},{... | collective-permute-start | bytes 82952 | tf_op jit(solution)/shard_map/ppermute | solution.py:44
  22.9 0.1 pad.4.clone
  23.0 0.4 copy.11
  23.4 1.2 %copy.12 = f32[72,24,4]{2,1,0:T(8,128)S(1)} copy(f32[72,24,4]{0,1,2:T(8,128)} %collective-permute-done.3) | data formatting | bytes 55296 | tf_op jit(solution)/shard_map/ppermute | solution.py:44
  24.5 1.9 %pad_maximum_fusion.padded = f32[72,24,384]{2,1,0:T(8,128)} fusion(f32[72,24,4]{2,1,0:T(8,128)S(1)} %copy.12, f32[72,24,4]{2,1,0:T(8,128)S(1)} %copy.11, f32[4,24,256]{2,1,0:T(8,128)S(1)} %collective-permute-done.1, f32[64,24,256]{2,1,0:T(8,128)S(1)} %maximum_bitcast_fusion, f32[4,24,256]{2,1,0:T(8,128)S(1)} %collective-permute-done, f32[384]{0:T(512)S(1)} %pad.4.clone), kind=kLoop, calls=%fused_computation | loop fusion | flops 3317760 | bytes 4480512 | tf_op jit(solution)/shard_map/concatenate | solution.py:369
  26.4 16.1 %powers.1 = (f32[64,80,256]{2,1,0:T(8,128)}, f32[96,128]{1,0:T(8,128)}) custom-call(f32[72,24,384]{2,1,0:T(8,128)} %pad_maximum_fusion.padded), custom_call_target="tpu_custom_call" | custom-call | tf_op jit(solution)/shard_map/powers/pallas_call | solution.py:117
  42.5 16.7 %total.2.gram = f32[96,128]{1,0:T(8,128)} custom-call(f32[96,128]{1,0:T(8,128)} %get-tuple-element.8.x_ref), custom_call_target="tpu_custom_call" | custom-call | tf_op jit(solution)/shard_map/total/pallas_call | solution.py:190
  59.2 19.1 %first.1 = (f32[80,128]{1,0:T(8,128)}, bf16[64,80,256]{2,1,0:T(8,128)(2,1)}, bf16[64,80,256]{2,1,0:T(8,128)(2,1)}, f32[96,128]{1,0:T(8,128)}) custom-call(f32[96,128]{1,0:T(8,128)} %total.2.gram, f32[64,80,256]{2,1,0:T(8,128)} %get-tuple-element.9.basis), custom_call_target="tpu_custom_call" | custom-call | tf_op jit(solution)/shard_map/first/pallas_call | solution.py:282
  78.4 14.2 %total.3.gram = f32[96,128]{1,0:T(8,128)} custom-call(f32[96,128]{1,0:T(8,128)} %get-tuple-element.10.x_ref), custom_call_target="tpu_custom_call" | custom-call | tf_op jit(solution)/shard_map/total/pallas_call | solution.py:190
  92.6 16.1 %second.1 = (f32[80,64,256]{2,1,0:T(8,128)}, f32[80,80]{1,0:T(8,128)}) custom-call(f32[96,128]{1,0:T(8,128)} %total.3.gram, f32[80,128]{1,0:T(8,128)} %get-tuple-element.11.upper_one, bf16[64,80,256]{2,1,0:T(8,128)(2,1)} %get-tuple-element.12.high, bf16[64,80,256]{2,1,0:T(8,128)(2,1)} %get-tuple-element.13.low), custom_call_target="tpu_custom_call" | custom-call | tf_op jit(solution)/shard_map/second/pallas_call | solution.py:335
  (6 shorter events, 0.1 us)
Async XLA Ops:
  4.8 7.1 %collective-permute-start = (f32[4,24,256]{2,1,0:T(8,128)S(1)}, f32[4,24,256]{2,1,0:T(8,128)S(1)}, u32[]{:S(2)}, u32[]{:S(2)}) collective-permute-start(f32[4,24,256]{2,1,0:T(8,128)S(1)} %get-tuple-element.16), channel_id=1, source_target_pairs={{0,4},{4,8},{8,12},{12,16},{16,20},{20,24},{24,28},{1,5},{5,9},{9,... | collective-permute-start | bytes 294920 | tf_op jit(solution)/shard_map/ppermute | solution.py:44
  9.7 6.5 %collective-permute-start.1 = (f32[4,24,256]{2,1,0:T(8,128)S(1)}, f32[4,24,256]{2,1,0:T(8,128)S(1)}, u32[]{:S(2)}, u32[]{:S(2)}) collective-permute-start(f32[4,24,256]{2,1,0:T(8,128)S(1)} %get-tuple-element.17), channel_id=1, source_target_pairs={{4,0},{8,4},{12,8},{16,12},{20,16},{24,20},{28,24},{5,1},{9,5},{13... | collective-permute-start | bytes 294920 | tf_op jit(solution)/shard_map/ppermute | solution.py:45
  17.6 5.3 %collective-permute-start.2 = (f32[72,24,4]{0,1,2:T(8,128)}, f32[72,24,4]{0,1,2:T(8,128)S(1)}, u32[]{:S(2)}, u32[]{:S(2)}) collective-permute-start(f32[72,24,4]{0,1,2:T(8,128)} %copy.9), channel_id=1, source_target_pairs={{1,0},{2,1},{3,2},{5,4},{6,5},{7,6},{9,8},{10,9},{11,10},{13,12},{... | collective-permute-start | bytes 82952 | tf_op jit(solution)/shard_map/ppermute | solution.py:45
  19.2 4.1 %collective-permute-start.3 = (f32[72,24,4]{0,1,2:T(8,128)S(1)}, f32[72,24,4]{0,1,2:T(8,128)}, u32[]{:S(2)}, u32[]{:S(2)}) collective-permute-start(f32[72,24,4]{0,1,2:T(8,128)S(1)} %copy.10), channel_id=1, source_target_pairs={{0,1},{1,2},{2,3},{4,5},{5,6},{6,7},{8,9},{9,10},{10,11},{12,13},{... | collective-permute-start | bytes 82952 | tf_op jit(solution)/shard_map/ppermute | solution.py:44

commit v2 on v1

--- a/solution.py
+++ b/solution.py
@@ -35,15 +35,142 @@
     return lax.dot_general(a, b, (((1,), (1,)), ((), ())), preferred_element_type=F32)
 
 
-def exchange(cells, axis, dim, width):
-    count = lax.axis_size(axis)
-    ends = count - 1
-    size = cells.shape[dim]
-    head = lax.slice_in_dim(cells, 0, width, axis=dim)
-    tail = lax.slice_in_dim(cells, size - width, size, axis=dim)
-    before = lax.ppermute(tail, axis, [(i, i + 1) for i in range(ends)])
-    after = lax.ppermute(head, axis, [(i + 1, i) for i in range(ends)])
-    return before, after
+FIELDS = B + 8
+SIDES = [(-1, 0), (1, 0), (0, -1), (0, 1), (-1, -1), (-1, 1), (1, -1), (1, 1)]
+
+
+def halo_kernel(nx, ny, right, center, couplings, out, packs, sides, corners, send, recv):
+    gx, gy = lax.axis_index("gx"), lax.axis_index("gy")
+    rows, cols = center.shape
+    last = cols - 128
+
+    def there(dx, dy):
+        ok = None
+        for test in ([gx > 0] if dx < 0 else [gx < nx - 1] if dx > 0 else []) + (
+            [gy > 0] if dy < 0 else [gy < ny - 1] if dy > 0 else []
+        ):
+            ok = test if ok is None else jnp.logical_and(ok, test)
+        return ok
+
+    def device(dx, dy):
+        return (lax.rem(gx + dx + nx, nx), lax.rem(gy + dy + ny, ny))
+
+    barrier = pltpu.get_barrier_semaphore()
+    for side in SIDES:
+        @pl.when(there(*side))
+        def _():
+            pl.semaphore_signal(barrier, inc=1, device_id=device(*side), device_id_type=MESH)
+
+    lane = lax.broadcasted_iota(jnp.int32, (FIELDS, 128), 1)
+    per = 128 // S
+    groups = rows // per
+    for g in range(rows // 8):
+        cut = pl.ds(8 * g, 8)
+        fields = jnp.concatenate(
+            [
+                right[:, cut, :],
+                (center[cut, :] - 5.0)[None],
+                couplings[:, cut, :],
+                jnp.zeros((FIELDS - B - 5, 8, cols), F32),
+            ],
+            axis=0,
+        )
+        out[S + 8 * g : S + 8 * g + 8, :, 0:cols] = jnp.swapaxes(fields, 0, 1)
+    for g in range(groups):
+        left = jnp.zeros((FIELDS, 128), F32)
+        far = jnp.zeros((FIELDS, 128), F32)
+        for j in range(per):
+            r = S + g * per + j
+            here = (lane >= S * j) & (lane < S * j + S)
+            a = out[r, :, 0:128]
+            z = out[r, :, last : last + 128]
+            left = jnp.where(here, pltpu.roll(a, S * j, 1) if j else a, left)
+            shift = (S * j + S) % 128
+            far = jnp.where(here, pltpu.roll(z, shift, 1) if shift else z, far)
+        packs[0, g] = left
+        packs[1, g] = far
+
+    near_x = (gx > 0).astype(jnp.int32) + (gx < nx - 1).astype(jnp.int32)
+    near_y = (gy > 0).astype(jnp.int32) + (gy < ny - 1).astype(jnp.int32)
+    pl.semaphore_wait(barrier, (1 + near_x) * (1 + near_y) - 1)
+
+    ends = groups - 1
+    core = pl.ds(0, cols)
+    ways = [
+        (out.at[pl.ds(S, S), :, core], out.at[pl.ds(rows + S, S), :, core]),
+        (out.at[pl.ds(rows, S), :, core], out.at[pl.ds(0, S), :, core]),
+        (packs.at[0], sides.at[1]),
+        (packs.at[1], sides.at[0]),
+        (packs.at[0, 0], corners.at[3]),
+        (packs.at[1, 0], corners.at[2]),
+        (packs.at[0, ends], corners.at[1]),
+        (packs.at[1, ends], corners.at[0]),
+    ]
+    copies = [
+        pltpu.make_async_remote_copy(
+            src_ref=src, dst_ref=dst, send_sem=send.at[i], recv_sem=recv.at[i],
+            device_id=device(*SIDES[i]), device_id_type=MESH,
+        )
+        for i, (src, dst) in enumerate(ways)
+    ]
+    for i, side in enumerate(SIDES):
+        @pl.when(there(*side))
+        def _():
+            copies[i].start()
+
+    for i, (dx, dy) in enumerate(SIDES):
+        dst = ways[i][1]
+        came = there(-dx, -dy)
+
+        @pl.when(jnp.logical_not(came))
+        def _():
+            dst[...] = jnp.zeros(dst.shape, F32)
+
+        @pl.when(came)
+        def _():
+            copies[i].wait_recv()
+
+    def halo(near, far, j):
+        a = pltpu.roll(far, (128 - S * j) % 128, 1) if j else far
+        shift = (128 - S - S * j) % 128
+        z = pltpu.roll(near, shift, 1) if shift else near
+        return jnp.where(lane < S, a, jnp.where(lane >= 128 - S, z, 0.0))
+
+    tail = slice(cols, cols + 128)
+    for g in range(groups):
+        near, far = sides[0, g], sides[1, g]
+        for j in range(per):
+            out[S + g * per + j, :, tail] = halo(near, far, j)
+    for i in range(S):
+        out[i, :, tail] = halo(corners[0], corners[1], per - S + i)
+        out[rows + S + i, :, tail] = halo(corners[2], corners[3], i)
+
+    for i, side in enumerate(SIDES):
+        @pl.when(there(*side))
+        def _():
+            copies[i].wait_send()
+
+
+def halo_fields(nx, ny, right_side, center, couplings):
+    rows, cols = center.shape
+    groups = rows * S // 128
+    return pl.pallas_call(
+        functools.partial(halo_kernel, nx, ny),
+        in_specs=[pl.BlockSpec(memory_space=pltpu.VMEM)] * 3,
+        out_specs=pl.BlockSpec(memory_space=pltpu.VMEM),
+        out_shape=jax.ShapeDtypeStruct((rows + 2 * S, FIELDS, cols + 128), F32),
+        scratch_shapes=[
+            pltpu.VMEM((2, groups, FIELDS, 128), F32),
+            pltpu.VMEM((2, groups, FIELDS, 128), F32),
+            pltpu.VMEM((4, FIELDS, 128), F32),
+            pltpu.SemaphoreType.DMA((8,)),
+            pltpu.SemaphoreType.DMA((8,)),
+        ],
+        compiler_params=pltpu.CompilerParams(
+            collective_id=2, has_side_effects=True, vmem_limit_bytes=VMEM_LIMIT
+        ),
+        name="halo",
+    )(right_side, center, couplings)
 
 
 def powers_kernel(rows, cols, chunk, padded, basis, gram, held, acc, levels):
@@ -209,25 +336,38 @@
     c = COLS
     row_id = lax.broadcasted_iota(jnp.int32, (c, 128), 0)
     lane_id = lax.broadcasted_iota(jnp.int32, (c, 128), 1)
-    work = jnp.concatenate([gram, (row_id == lane_id).astype(F32)], axis=1)
-    tiles = [work[8 * t : 8 * t + 8] for t in range(c // 8)]
-    sub = lax.broadcasted_iota(jnp.int32, (8, 1), 0)
-    for k in range(c):
-        t0, s0 = divmod(k, 8)
-        row = tiles[t0][s0 : s0 + 1]
-        pivot = row[:, k : k + 1]
-        scale = 1.0 / jnp.sqrt(pivot)
-        row = row * scale
-        for t in range(t0, c // 8):
-            mult = tiles[t][:, k : k + 1] * scale
-            if t == t0:
-                mult = jnp.where(sub > s0, mult, 0.0)
-                tiles[t] = jnp.where(sub == s0, row, tiles[t] - mult * row)
-            else:
-                tiles[t] = tiles[t] - mult * row
-    done = jnp.concatenate(tiles, axis=0)
-    upper = jnp.where(lane_id >= row_id, done[:, 0:128], 0.0)
-    return upper, done[:, 128:256]
+    eye = (row_id == lane_id).astype(F32)
+    upper = [gram[8 * t : 8 * t + 8] for t in range(c // 8)]
+    lower = [eye[8 * t : 8 * t + 8] for t in range(c // 8)]
+    sub = lax.broadcasted_iota(jnp.int32, (8, 128), 0)
+    scales = []
+    for b in range(c // 8):
+        later = range(b, c // 8)
+        columns = {
+            t: [
+                jnp.broadcast_to(upper[t][:, 8 * b + j : 8 * b + j + 1], (8, 128))
+                for j in range(8)
+            ]
+            for t in later
+        }
+        scale = jnp.zeros((8, 128), F32)
+        for j in range(8):
+            heads = [columns[b][i][j : j + 1] for i in range(8)]
+            inv = 1.0 / heads[j]
+            scale = jnp.where(sub == j, heads[j], scale)
+            row_u, row_l = upper[b][j : j + 1], lower[b][j : j + 1]
+            for t in later:
+                mult = columns[t][j] * inv
+                if t == b:
+                    mult = jnp.where(sub > j, mult, 0.0)
+                for i in range(j + 1, 8):
+                    columns[t][i] = columns[t][i] - mult * heads[i]
+                upper[t] = upper[t] - mult * row_u
+                lower[t] = lower[t] - mult * row_l
+        scales.append(scale)
+    scale = 1.0 / jnp.sqrt(jnp.concatenate(scales, axis=0))
+    up = jnp.concatenate(upper, axis=0) * scale
+    return jnp.where(lane_id >= row_id, up, 0.0), jnp.concatenate(lower, axis=0) * scale
 
 
 def spread(parts):
@@ -358,16 +498,7 @@
 def on_device(nx, ny, right_side, center, couplings):
     rows, cols = center.shape
     norm = math.sqrt(rows * cols * nx * ny)
-    fields = jnp.concatenate(
-        [right_side, (center - 5.0)[None], couplings, jnp.zeros((3, rows, cols), F32)], 0
-    )
-    fields = jnp.swapaxes(fields, 0, 1)
-    up, down = exchange(fields, "gx", 0, S)
-    fields = jnp.concatenate([up, fields, down], 0)
-    left, right = exchange(fields, "gy", 2, S)
-    gap = jnp.zeros(fields.shape[:2] + (128 - 2 * S,), F32)
-    padded = jnp.concatenate([fields, right, gap, left], 2)
-
+    padded = halo_fields(nx, ny, right_side, center, couplings)
     pad_rows = -(-COLS // (8 * ny)) * 8 * ny
     basis, gram = powers(padded, rows, cols, pad_rows)
     gram = total(gram, nx, ny, 1)

time: 110 us -> 83.6 us (0.76)
  starting transfers between devices: 11.1 us -> 0 us
  local copies, waits for them, and re-layouts: 6.32 us -> 0 us
  waiting for transfers between devices: 5.22 us -> 0 us
  other arithmetic: 3.06 us -> 0 us
    pallas_call x0 -> x1, Pallas kernels: none -> 12 us  [halo_fields(): pl.pallas_call(functools.partial(halo_kernel, nx, ny), in_specs=[pl.Block...]
    ppermute x4 -> x0, starting transfers between devices: 11.1 us -> none  [the longest x2 8.52 us: exchange(): before = lax.ppermute(tail, axis, [(i, i + 1) for i in range(ends)])]
    pallas_call x1, Pallas kernels: 16.1 us -> 10.4 us  [second(): pl.pallas_call(functools.partial(second_kernel, chunk, norm), grid=(rows...]
    pallas_call x1, Pallas kernels: 19.1 us -> 13.5 us  [first(): pl.pallas_call(functools.partial(first_kernel, chunk), grid=(rows // chun...]
    ppermute x4 -> x0, waiting for transfers between devices: 5.22 us -> none  [the longest x2 4.32 us: exchange(): after = lax.ppermute(head, axis, [(i + 1, i) for i in range(ends)])]
    unnamed x2 -> x0, local copies, waits for them, and re-layouts: 2.96 us -> none
    concatenate x2 -> x0, other arithmetic: 2 us -> none  [the longest x1 1.88 us: on_device(): padded = jnp.concatenate([fields, right, gap, left], 2)]
    slice x4 -> x0, local copies, waits for them, and re-layouts: 1.6 us -> none  [the longest x2 1.26 us: exchange(): head = lax.slice_in_dim(cells, 0, width, axis=dim)]
  transfers between devices with their start and end apart: 4 -> 0, of which waited for: 2 -> 0; matrix products, arithmetic and copies ran while one was open for 1% -> 0% of each run, Pallas kernels for 0% -> 0%
where the time goes in v2:
time: 83.6 us; the launch traced here: 82.9 us
  Pallas kernels  82.3 us (98%)
    pallas_call x2, Pallas kernels, total(): pl.pallas_call(functools.partial(total_kernel, nx, ny, piece), in_specs=[...  30.2 us
    pallas_call x1, Pallas kernels, powers(): pl.pallas_call(functools.partial(powers_kernel, rows, cols, chunk), grid=...  16.1 us
    pallas_call x1, Pallas kernels, first(): pl.pallas_call(functools.partial(first_kernel, chunk), grid=(rows // chun...  13.5 us
    pallas_call x1, Pallas kernels, halo_fields(): pl.pallas_call(functools.partial(halo_kernel, nx, ny), in_specs=[pl.Block...  12 us
    pallas_call x1, Pallas kernels, second(): pl.pallas_call(functools.partial(second_kernel, chunk, norm), grid=(rows...  10.4 us

profile of v2, /device:TPU:0, one launch (start us, length us, event | category | flops | bytes accessed | tf_op | source)
XLA Modules:
  0.0 82.9 jit_solution(3205144463341516404)
XLA Ops:
  0.6 12.0 %halo.1.padded = f32[72,24,384]{2,1,0:T(8,128)} custom-call(f32[16,64,256]{2,1,0:T(8,128)} %right.1, f32[64,256]{1,0:T(8,128)} %center.1, f32[4,64,256]{2,1,0:T(8,128)} %couplings.1), custom_call_target="tpu_custom_call" | custom-call | tf_op jit(solution)/shard_map/halo/pallas_call | solution.py:157
  12.6 16.1 %powers.1 = (f32[64,80,256]{2,1,0:T(8,128)}, f32[96,128]{1,0:T(8,128)}) custom-call(f32[72,24,384]{2,1,0:T(8,128)} %halo.1.padded), custom_call_target="tpu_custom_call" | custom-call | tf_op jit(solution)/shard_map/powers/pallas_call | solution.py:244
  28.7 16.1 %total.2.gram = f32[96,128]{1,0:T(8,128)} custom-call(f32[96,128]{1,0:T(8,128)} %get-tuple-element.8.x_ref), custom_call_target="tpu_custom_call" | custom-call | tf_op jit(solution)/shard_map/total/pallas_call | solution.py:317
  44.8 13.5 %first.1 = (f32[80,128]{1,0:T(8,128)}, bf16[64,80,256]{2,1,0:T(8,128)(2,1)}, bf16[64,80,256]{2,1,0:T(8,128)(2,1)}, f32[96,128]{1,0:T(8,128)}) custom-call(f32[96,128]{1,0:T(8,128)} %total.2.gram, f32[64,80,256]{2,1,0:T(8,128)} %get-tuple-element.9.basis), custom_call_target="tpu_custom_call" | custom-call | tf_op jit(solution)/shard_map/first/pallas_call | solution.py:422
  58.4 14.1 %total.3.gram = f32[96,128]{1,0:T(8,128)} custom-call(f32[96,128]{1,0:T(8,128)} %get-tuple-element.10.x_ref), custom_call_target="tpu_custom_call" | custom-call | tf_op jit(solution)/shard_map/total/pallas_call | solution.py:317
  72.5 10.4 %second.1 = (f32[80,64,256]{2,1,0:T(8,128)}, f32[80,80]{1,0:T(8,128)}) custom-call(f32[96,128]{1,0:T(8,128)} %total.3.gram, f32[80,128]{1,0:T(8,128)} %get-tuple-element.11.upper_one, bf16[64,80,256]{2,1,0:T(8,128)(2,1)} %get-tuple-element.12.high, bf16[64,80,256]{2,1,0:T(8,128)(2,1)} %get-tuple-element.13.low), custom_call_target="tpu_custom_call" | custom-call | tf_op jit(solution)/shard_map/second/pallas_call | solution.py:475

commit v3 on v2

--- a/solution.py
+++ b/solution.py
@@ -173,8 +173,89 @@
     )(right_side, center, couplings)
 
 
-def powers_kernel(rows, cols, chunk, padded, basis, gram, held, acc, levels):
+class Total:
+    def __init__(self, nx, ny):
+        self.nx, self.ny = nx, ny
+        self.pad_rows = -(-COLS // (8 * ny)) * 8 * ny
+        self.piece = self.pad_rows // ny
+
+    def scratch(self):
+        nx, ny = self.nx, self.ny
+        return [
+            pltpu.VMEM((self.pad_rows, 128), F32),
+            pltpu.VMEM((self.pad_rows, 128), F32),
+            pltpu.VMEM((ny, self.piece, 128), F32),
+            pltpu.VMEM((nx, self.piece, 128), F32),
+            pltpu.SemaphoreType.DMA((max(nx, ny),)),
+            pltpu.SemaphoreType.DMA((ny,)),
+            pltpu.SemaphoreType.DMA((nx,)),
+            pltpu.SemaphoreType.DMA((ny,)),
+        ]
+
+    def peers(self):
+        nx, ny = self.nx, self.ny
+        gx, gy = lax.axis_index("gx"), lax.axis_index("gy")
+        rows = [(gx, lax.rem(gy + d, ny)) for d in range(1, ny)]
+        columns = [(lax.rem(gx + d, nx), gy) for d in range(1, nx)]
+        return gx, gy, rows, columns
+
+    def greet(self):
+        _, _, rows, columns = self.peers()
+        barrier = pltpu.get_barrier_semaphore()
+        for peer in rows + columns:
+            pl.semaphore_signal(barrier, inc=1, device_id=peer, device_id_type=MESH)
+
+    def run(self, scratch):
+        x_ref, out_ref, got_row, got_col, send, r1, r2, r3 = scratch
+        gx, gy, rows, columns = self.peers()
+        pl.semaphore_wait(pltpu.get_barrier_semaphore(), len(rows) + len(columns))
+
+        def push(src, dst, index, sem, peer):
+            copy = pltpu.make_async_remote_copy(
+                src_ref=src, dst_ref=dst, send_sem=send.at[index], recv_sem=sem,
+                device_id=peer, device_id_type=MESH,
+            )
+            copy.start()
+            return copy
+
+        def part(i):
+            return pl.ds(pl.multiple_of(i * self.piece, 8), self.piece)
+
+        copies = [
+            push(x_ref.at[part(peer[1])], got_row.at[gy], i, r1.at[i], peer)
+            for i, peer in enumerate(rows)
+        ]
+        got_row[gy] = x_ref[part(gy)]
+        for copy in copies:
+            copy.wait()
+        held = got_row[0]
+        for i in range(1, self.ny):
+            held = held + got_row[i]
+        got_col[gx] = held
+        copies = [
+            push(got_col.at[gx], got_col.at[gx], i, r2.at[i], peer)
+            for i, peer in enumerate(columns)
+        ]
+        for copy in copies:
+            copy.wait()
+        held = got_col[0]
+        for i in range(1, self.nx):
+            held = held + got_col[i]
+        out_ref[part(gy)] = held
+        copies = [
+            push(out_ref.at[part(gy)], out_ref.at[part(gy)], i, r3.at[i], peer)
+            for i, peer in enumerate(rows)
+        ]
+        for copy in copies:
+            copy.wait()
+
+
+def powers_kernel(total, rows, cols, chunk, padded, basis, gram, held, acc, levels, *scratch):
     step = pl.program_id(0)
+
+    @pl.when(step == 0)
+    def _():
+        total.greet()
 
     def apply(power, r):
         if power == 1:
@@ -234,15 +315,18 @@
             return a[i * c : i * c + c, j * c : j * c + c]
 
         small = block(0, 2) + block(2, 0) + block(1, 1)
-        total = block(0, 0) + ((block(0, 1) + block(1, 0)) + small)
-        gram[...] = jnp.zeros_like(gram)
-        gram[0:c, 0:c] = total
-
-
-def powers(padded, rows, cols, pad_rows):
+        own = scratch[0]
+        own[...] = jnp.zeros_like(own)
+        own[0:c, 0:c] = block(0, 0) + ((block(0, 1) + block(1, 0)) + small)
+        total.run(scratch)
+        gram[...] = scratch[1][...]
+
+
+def powers(total, padded, rows, cols):
+    pad_rows = total.pad_rows
     chunk = 8
     return pl.pallas_call(
-        functools.partial(powers_kernel, rows, cols, chunk),
+        functools.partial(powers_kernel, total, rows, cols, chunk),
         grid=(rows // chunk,),
         in_specs=[pl.BlockSpec(padded.shape, lambda i: (0, 0, 0))],
         out_specs=[
@@ -257,79 +341,13 @@
             pltpu.VMEM((rows, COLS, cols), F32),
             pltpu.VMEM((3 * COLS, 3 * COLS), F32),
             pltpu.VMEM((2, padded.shape[0], B, padded.shape[2]), F32),
-        ],
-        compiler_params=pltpu.CompilerParams(vmem_limit_bytes=VMEM_LIMIT),
+        ]
+        + total.scratch(),
+        compiler_params=pltpu.CompilerParams(
+            collective_id=0, has_side_effects=True, vmem_limit_bytes=VMEM_LIMIT
+        ),
         name="powers",
     )(padded)
-
-
-def total_kernel(nx, ny, piece, x_ref, out_ref, got_row, got_col, send, r1, r2, r3):
-    gx, gy = lax.axis_index("gx"), lax.axis_index("gy")
-    barrier = pltpu.get_barrier_semaphore()
-    rows = [(gx, lax.rem(gy + d, ny)) for d in range(1, ny)]
-    columns = [(lax.rem(gx + d, nx), gy) for d in range(1, nx)]
-    for peer in rows + columns:
-        pl.semaphore_signal(barrier, inc=1, device_id=peer, device_id_type=MESH)
-    pl.semaphore_wait(barrier, len(rows) + len(columns))
-
-    def push(src, dst, index, sem, peer):
-        copy = pltpu.make_async_remote_copy(
-            src_ref=src, dst_ref=dst, send_sem=send.at[index], recv_sem=sem,
-            device_id=peer, device_id_type=MESH,
-        )
-        copy.start()
-        return copy
-
-    def part(i):
-        return pl.ds(pl.multiple_of(i * piece, 8), piece)
-
-    copies = [
-        push(x_ref.at[part(peer[1])], got_row.at[gy], i, r1.at[i], peer)
-        for i, peer in enumerate(rows)
-    ]
-    got_row[gy] = x_ref[part(gy)]
-    for copy in copies:
-        copy.wait()
-    held = got_row[0]
-    for i in range(1, ny):
-        held = held + got_row[i]
-    got_col[gx] = held
-    copies = [
-        push(got_col.at[gx], got_col.at[gx], i, r2.at[i], peer) for i, peer in enumerate(columns)
-    ]
-    for copy in copies:
-        copy.wait()
-    held = got_col[0]
-    for i in range(1, nx):
-        held = held + got_col[i]
-    out_ref[part(gy)] = held
-    copies = [
-        push(out_ref.at[part(gy)], out_ref.at[part(gy)], i, r3.at[i], peer)
-        for i, peer in enumerate(rows)
-    ]
-    for copy in copies:
-        copy.wait()
-
-
-def total(x, nx, ny, ident):
-    piece = x.shape[0] // ny
-    most = max(nx, ny) - 1
-    return pl.pallas_call(
-        functools.partial(total_kernel, nx, ny, piece),
-        in_specs=[pl.BlockSpec(memory_space=pltpu.VMEM)],
-        out_specs=pl.BlockSpec(memory_space=pltpu.VMEM),
-        out_shape=jax.ShapeDtypeStruct(x.shape, F32),
-        scratch_shapes=[
-            pltpu.VMEM((ny, piece, 128), F32),
-            pltpu.VMEM((nx, piece, 128), F32),
-            pltpu.SemaphoreType.DMA((most,)),
-            pltpu.SemaphoreType.DMA((max(ny - 1, 1),)),
-            pltpu.SemaphoreType.DMA((max(nx - 1, 1),)),
-            pltpu.SemaphoreType.DMA((max(ny - 1, 1),)),
-        ],
-        compiler_params=pltpu.CompilerParams(collective_id=ident, has_side_effects=True),
-        name="total",
-    )(x)
 
 
 def eliminate(gram):
@@ -354,6 +372,7 @@
         for j in range(8):
             heads = [columns[b][i][j : j + 1] for i in range(8)]
             inv = 1.0 / heads[j]
+            inv = inv * (2.0 - heads[j] * inv)
             scale = jnp.where(sub == j, heads[j], scale)
             row_u, row_l = upper[b][j : j + 1], lower[b][j : j + 1]
             for t in later:
@@ -365,7 +384,9 @@
                 upper[t] = upper[t] - mult * row_u
                 lower[t] = lower[t] - mult * row_l
         scales.append(scale)
-    scale = 1.0 / jnp.sqrt(jnp.concatenate(scales, axis=0))
+    pivots = jnp.concatenate(scales, axis=0)
+    scale = 1.0 / jnp.sqrt(pivots)
+    scale = scale * (1.5 - 0.5 * (pivots * scale) * scale)
     up = jnp.concatenate(upper, axis=0) * scale
     return jnp.where(lane_id >= row_id, up, 0.0), jnp.concatenate(lower, axis=0) * scale
 
@@ -380,11 +401,12 @@
     return wide.astype(BF16)
 
 
-def first_kernel(chunk, gram, basis, upper_ref, high, low, gram_out, left, acc):
+def first_kernel(total, chunk, gram, basis, upper_ref, high, low, gram_out, left, acc, *scratch):
     step = pl.program_id(0)
 
     @pl.when(step == 0)
     def _():
+        total.greet()
         acc[...] = jnp.zeros_like(acc)
         upper, inverse = eliminate(gram[0:COLS, :])
         upper_ref[...] = upper
@@ -410,17 +432,20 @@
     def _():
         c = COLS
         a = acc[...]
-        gram_out[...] = jnp.zeros_like(gram_out)
-        gram_out[0:c, 0:c] = a[0:c, 0:c] + (
+        own = scratch[0]
+        own[...] = jnp.zeros_like(own)
+        own[0:c, 0:c] = a[0:c, 0:c] + (
             (a[0:c, c : 2 * c] + a[c : 2 * c, 0:c]) + a[c : 2 * c, c : 2 * c]
         )
-
-
-def first(gram, basis):
+        total.run(scratch)
+        gram_out[...] = scratch[1][...]
+
+
+def first(total, gram, basis):
     rows, _, cols = basis.shape
     chunk = 8
     return pl.pallas_call(
-        functools.partial(first_kernel, chunk),
+        functools.partial(first_kernel, total, chunk),
         grid=(rows // chunk,),
         in_specs=[
             pl.BlockSpec(gram.shape, lambda i: (0, 0)),
@@ -441,8 +466,11 @@
         scratch_shapes=[
             pltpu.VMEM((2, COLS, 256), BF16),
             pltpu.VMEM((2 * COLS, 2 * COLS), F32),
-        ],
-        compiler_params=pltpu.CompilerParams(vmem_limit_bytes=VMEM_LIMIT),
+        ]
+        + total.scratch(),
+        compiler_params=pltpu.CompilerParams(
+            collective_id=1, has_side_effects=True, vmem_limit_bytes=VMEM_LIMIT
+        ),
         name="first",
     )(gram, basis)
 
@@ -499,11 +527,9 @@
     rows, cols = center.shape
     norm = math.sqrt(rows * cols * nx * ny)
     padded = halo_fields(nx, ny, right_side, center, couplings)
-    pad_rows = -(-COLS // (8 * ny)) * 8 * ny
-    basis, gram = powers(padded, rows, cols, pad_rows)
-    gram = total(gram, nx, ny, 1)
-    upper_one, high, low, gram = first(gram, basis)
-    gram = total(gram, nx, ny, 1)
+    total = Total(nx, ny)
+    basis, gram = powers(total, padded, rows, cols)
+    upper_one, high, low, gram = first(total, gram, basis)
     return second(gram, upper_one, high, low, norm)
 
 

time: 83.6 us -> 76.8 us (0.919)
  Pallas kernels: 82.3 us -> 75.6 us
    pallas_call x4 -> x2, Pallas kernels: 59.8 us -> 52.9 us  [the longest x1 29.3 us: powers(): pl.pallas_call(functools.partial(powers_kernel, total, rows, cols, chunk)...]
where the time goes in v3:
time: 76.8 us; the launch traced here: 76.3 us
  Pallas kernels  75.6 us (98%)
    pallas_call x1, Pallas kernels, powers(): pl.pallas_call(functools.partial(powers_kernel, total, rows, cols, chunk)...  29.3 us
    pallas_call x1, Pallas kernels, first(): pl.pallas_call(functools.partial(first_kernel, total, chunk), grid=(rows...  23.6 us
    pallas_call x1, Pallas kernels, halo_fields(): pl.pallas_call(functools.partial(halo_kernel, nx, ny), in_specs=[pl.Block...  12 us
    pallas_call x1, Pallas kernels, second(): pl.pallas_call(functools.partial(second_kernel, chunk, norm), grid=(rows...  10.7 us

profile of v3, /device:TPU:0, one launch (start us, length us, event | category | flops | bytes accessed | tf_op | source)
XLA Modules:
  0.0 76.3 jit_solution(20557338359845014)
XLA Ops:
  0.6 12.0 %halo.1.padded = f32[72,24,384]{2,1,0:T(8,128)} custom-call(f32[16,64,256]{2,1,0:T(8,128)} %right.1, f32[64,256]{1,0:T(8,128)} %center.1, f32[4,64,256]{2,1,0:T(8,128)} %couplings.1), custom_call_target="tpu_custom_call" | custom-call | tf_op jit(solution)/shard_map/halo/pallas_call | solution.py:157
  12.6 29.3 %powers.1 = (f32[64,80,256]{2,1,0:T(8,128)}, f32[96,128]{1,0:T(8,128)}) custom-call(f32[72,24,384]{2,1,0:T(8,128)} %halo.1.padded), custom_call_target="tpu_custom_call" | custom-call | tf_op jit(solution)/shard_map/powers/pallas_call | solution.py:328
  42.0 23.6 %first.1 = (f32[80,128]{1,0:T(8,128)}, bf16[64,80,256]{2,1,0:T(8,128)(2,1)}, bf16[64,80,256]{2,1,0:T(8,128)(2,1)}, f32[96,128]{1,0:T(8,128)}) custom-call(f32[96,128]{1,0:T(8,128)} %get-tuple-element.8.gram, f32[64,80,256]{2,1,0:T(8,128)} %get-tuple-element.9.basis), custom_call_target="tpu_custom_call" | custom-call | tf_op jit(solution)/shard_map/first/pallas_call | solution.py:447
  65.6 10.7 %second.1 = (f32[80,64,256]{2,1,0:T(8,128)}, f32[80,80]{1,0:T(8,128)}) custom-call(f32[96,128]{1,0:T(8,128)} %get-tuple-element.10.gram, f32[80,128]{1,0:T(8,128)} %get-tuple-element.11.upper_one, bf16[64,80,256]{2,1,0:T(8,128)(2,1)} %get-tuple-element.12.high, bf16[64,80,256]{2,1,0:T(8,128)(2,1)} %get-tuple-element.13.low), custom_call_target="tpu_custom_call" | custom-call | tf_op jit(solution)/shard_map/second/pallas_call | solution.py:503

commit v4 on v3

--- a/solution.py
+++ b/solution.py
@@ -283,7 +283,7 @@
             held[r, 0:B, :] = padded[r + S, 0:B, 0:cols]
             return carry
 
-        lax.fori_loop(0, rows, copy_row, 0, unroll=4)
+        lax.fori_loop(0, rows, copy_row, 0, unroll=8)
         for power in range(1, S + 1):
             for r in list(range(power, S)) + list(range(rows + S, rows + 2 * S - power)):
                 levels[power % 2, r] = apply(power, r)
@@ -295,7 +295,7 @@
                 held[r, B * power : B * power + B, :] = out[:, 0:cols]
                 return carry
 
-            lax.fori_loop(0, rows, row, 0, unroll=4)
+            lax.fori_loop(0, rows, row, 0, unroll=8)
 
     basis[...] = held[pl.ds(step * chunk, chunk)]
     part = None
@@ -324,7 +324,7 @@
 
 def powers(total, padded, rows, cols):
     pad_rows = total.pad_rows
-    chunk = 8
+    chunk = 32
     return pl.pallas_call(
         functools.partial(powers_kernel, total, rows, cols, chunk),
         grid=(rows // chunk,),
@@ -443,7 +443,7 @@
 
 def first(total, gram, basis):
     rows, _, cols = basis.shape
-    chunk = 8
+    chunk = 32
     return pl.pallas_call(
         functools.partial(first_kernel, total, chunk),
         grid=(rows // chunk,),
@@ -499,7 +499,7 @@
 
 def second(gram, upper_one, high, low, norm):
     rows, _, cols = high.shape
-    chunk = 8
+    chunk = 32
     return pl.pallas_call(
         functools.partial(second_kernel, chunk, norm),
         grid=(rows // chunk,),

time: 76.8 us -> 67.1 us (0.87)
  Pallas kernels: 75.6 us -> 66.2 us
    pallas_call x1, Pallas kernels: 29.3 us -> 25.5 us  [powers(): pl.pallas_call(functools.partial(powers_kernel, total, rows, cols, chunk)...]
    pallas_call x1, Pallas kernels: 10.7 us -> 7.69 us  [second(): pl.pallas_call(functools.partial(second_kernel, chunk, norm), grid=(rows...]
    pallas_call x1, Pallas kernels: 23.6 us -> 21.1 us  [first(): pl.pallas_call(functools.partial(first_kernel, total, chunk), grid=(rows...]
where the time goes in v4:
time: 67.1 us; the launch traced here: 66.9 us
  Pallas kernels  66.2 us (99%)
    pallas_call x1, Pallas kernels, powers(): pl.pallas_call(functools.partial(powers_kernel, total, rows, cols, chunk)...  25.5 us
    pallas_call x1, Pallas kernels, first(): pl.pallas_call(functools.partial(first_kernel, total, chunk), grid=(rows...  21.1 us
    pallas_call x1, Pallas kernels, halo_fields(): pl.pallas_call(functools.partial(halo_kernel, nx, ny), in_specs=[pl.Block...  12 us
    pallas_call x1, Pallas kernels, second(): pl.pallas_call(functools.partial(second_kernel, chunk, norm), grid=(rows...  7.69 us

profile of v4, /device:TPU:0, one launch (start us, length us, event | category | flops | bytes accessed | tf_op | source)
XLA Modules:
  0.0 66.9 jit_solution(15697909050431159423)
XLA Ops:
  0.6 12.0 %halo.1.padded = f32[72,24,384]{2,1,0:T(8,128)} custom-call(f32[16,64,256]{2,1,0:T(8,128)} %right.1, f32[64,256]{1,0:T(8,128)} %center.1, f32[4,64,256]{2,1,0:T(8,128)} %couplings.1), custom_call_target="tpu_custom_call" | custom-call | tf_op jit(solution)/shard_map/halo/pallas_call | solution.py:157
  12.6 25.5 %powers.1 = (f32[64,80,256]{2,1,0:T(8,128)}, f32[96,128]{1,0:T(8,128)}) custom-call(f32[72,24,384]{2,1,0:T(8,128)} %halo.1.padded), custom_call_target="tpu_custom_call" | custom-call | tf_op jit(solution)/shard_map/powers/pallas_call | solution.py:328
  38.1 21.1 %first.1 = (f32[80,128]{1,0:T(8,128)}, bf16[64,80,256]{2,1,0:T(8,128)(2,1)}, bf16[64,80,256]{2,1,0:T(8,128)(2,1)}, f32[96,128]{1,0:T(8,128)}) custom-call(f32[96,128]{1,0:T(8,128)} %get-tuple-element.8.gram, f32[64,80,256]{2,1,0:T(8,128)} %get-tuple-element.9.basis), custom_call_target="tpu_custom_call" | custom-call | tf_op jit(solution)/shard_map/first/pallas_call | solution.py:447
  59.2 7.7 %second.1 = (f32[80,64,256]{2,1,0:T(8,128)}, f32[80,80]{1,0:T(8,128)}) custom-call(f32[96,128]{1,0:T(8,128)} %get-tuple-element.10.gram, f32[80,128]{1,0:T(8,128)} %get-tuple-element.11.upper_one, bf16[64,80,256]{2,1,0:T(8,128)(2,1)} %get-tuple-element.12.high, bf16[64,80,256]{2,1,0:T(8,128)(2,1)} %get-tuple-element.13.low), custom_call_target="tpu_custom_call" | custom-call | tf_op jit(solution)/shard_map/second/pallas_call | solution.py:503
